TPU v7x, 256 devices: a whole 4x4x8 slice. The times are simulated.
256 devices in a mesh: sub: 16 (over y_lo, z), bl: 16 (over x, y_hi, core).
Axes of the slice: x: 4, y: 4 (y_hi: 2, y_lo: 2; y = y_hi * 2 + y_lo), z: 8, core: 2. Of those that a mesh axis runs over, the one named last changes fastest.
Arguments:
- coherency: bfloat16 [128, 32768, 128], P('sub', 'bl'), may hold values from -1.5 to 1.5
- visibility: float32 [2, 128, 32768], P(None, 'sub', 'bl'), may hold values from -24 to 24
- stations: int32 [2, 32768], P(None, 'bl'), may hold values from 0 to 511, as said below
- gains: float32 [128, 512, 128], P('sub', 'bl'), may hold values from -6 to 6
- dual: float32 [128, 512, 128], P('sub', 'bl'), may hold values from -3 to 3
- coeffs: float32 [4, 512, 128], P(None, 'bl'), may hold values from -6 to 6
- penalty: int32 [128], replicated, may hold values from 1 to 8
Outputs:
- new_gains: float32 [128, 512, 128], P('sub', 'bl')
- new_dual: float32 [128, 512, 128], P('sub', 'bl')
- new_coeffs: float32 [4, 512, 128], P(None, 'bl')
Inputs may be any that keep to these rules, and one draw needn't show every extreme that they name: The two stations of every baseline differ.
All inputs are finite; a program needn't handle non-finite values.
Results may differ from a plain program's by a relative error of at most 0.0028.
Values sent between devices are 32-bit elements; how exact they have to be, the bound alone decides.
A program may use at most 128 MiB of HBM per device.

v0:
```python
import math

import jax
import jax.numpy as jnp
from jax import lax
from jax.sharding import PartitionSpec as P


def bernstein_table(count, terms):
    position = (jnp.arange(count).astype(jnp.float32) + 0.5) / count
    degree = terms - 1
    return jnp.stack(
        [
            math.comb(degree, order) * position**order * (1.0 - position) ** (degree - order)
            for order in range(terms)
        ]
    )


def channel_terms(coh, vis_re, vis_im, gain_table, lower_edge, right_end):
    half_width = gain_table.shape[-1] // 2
    near = jnp.take(gain_table, lower_edge, axis=-2)
    far = jnp.take(gain_table, right_end, axis=-2)
    near_re, near_im = (near[..., :half_width], near[..., half_width:])
    far_re, far_im = (far[..., :half_width], far[..., half_width:])
    coh_f = coh.astype(jnp.float32)
    coh_re, coh_im = (coh_f[..., :half_width], coh_f[..., half_width:])
    hat_re = coh_re * far_re + coh_im * far_im
    hat_im = coh_im * far_re - coh_re * far_im
    model_re = near_re * hat_re - near_im * hat_im
    model_im = near_re * hat_im + near_im * hat_re
    resid_re = vis_re - jnp.sum(model_re, axis=-1)
    resid_im = vis_im - jnp.sum(model_im, axis=-1)
    target_re = resid_re[..., None] + model_re
    target_im = resid_im[..., None] + model_im
    tilde_re = coh_re * near_re - coh_im * near_im
    tilde_im = coh_re * near_im + coh_im * near_re
    terms_left = jnp.concatenate(
        [
            target_re * hat_re + target_im * hat_im,
            target_im * hat_re - target_re * hat_im,
            hat_re * hat_re + hat_im * hat_im,
        ],
        axis=-1,
    )
    terms_right = jnp.concatenate(
        [
            target_re * tilde_re + target_im * tilde_im,
            target_re * tilde_im - target_im * tilde_re,
            tilde_re * tilde_re + tilde_im * tilde_im,
        ],
        axis=-1,
    )
    return (terms_left.astype(jnp.bfloat16), terms_right.astype(jnp.bfloat16))


def gain_update(normals, dual, prior, weights):
    width_two = dual.shape[-1]
    numerator = normals[..., :width_two]
    squares = normals[..., width_two:]
    denominator = jnp.concatenate([squares, squares], axis=-1) + weights[:, None, None]
    return (numerator + weights[:, None, None] * (prior - dual)) / denominator


def poly_solve(lower, moments):
    terms = moments.shape[0]
    forward = []
    for row in range(terms):
        value = moments[row]
        for col in range(row):
            value = value - lower[row, col] * forward[col]
        forward.append(value / lower[row, row])
    backward = [None] * terms
    for row in range(terms - 1, -1, -1):
        value = forward[row]
        for col in range(row + 1, terms):
            value = value - lower[col, row] * backward[col]
        backward[row] = value / lower[row, row]
    return jnp.stack(backward)


def shards(coherency, visibility, stations, gains, dual, coeffs, penalty):
    full_gains = lax.all_gather(gains, "bl", axis=1, tiled=True)
    channels, station_count, width_two = full_gains.shape
    own_rows = gains.shape[1]
    lower_edge = stations[0]
    right_end = stations[1]
    terms_left, terms_right = channel_terms(
        coherency, visibility[0], visibility[1], full_gains, lower_edge, right_end
    )
    rows = jnp.arange(lax.axis_size("bl") * own_rows)
    hot_left = (lower_edge[None, :] == rows[:, None]).astype(jnp.bfloat16)
    hot_right = (right_end[None, :] == rows[:, None]).astype(jnp.bfloat16)
    summed = jnp.einsum("sb,fbc->sfc", hot_left, terms_left, preferred_element_type=jnp.float32)
    summed = summed + jnp.einsum(
        "sb,fbc->sfc", hot_right, terms_right, preferred_element_type=jnp.float32
    )
    own_normals = lax.psum_scatter(
        summed.reshape(lax.axis_size("bl") * own_rows, -1), "bl", scatter_dimension=0, tiled=True
    )
    normals = jnp.transpose(own_normals.reshape(own_rows, channels, -1), (1, 0, 2))
    total_channels = channels * lax.axis_size("sub")
    bernstein = bernstein_table(total_channels, coeffs.shape[0])
    weights_all = 4.0 * penalty.astype(jnp.float32)
    weighted = bernstein * weights_all[None, :]
    gram_matrix = jnp.dot(weighted, bernstein.T, precision=lax.Precision.HIGHEST)
    factor_lower = jnp.linalg.cholesky(gram_matrix)
    channel_start = lax.axis_index("sub") * channels
    local_basis = lax.dynamic_slice_in_dim(bernstein, channel_start, channels, 1)
    local_weighted = lax.dynamic_slice_in_dim(weighted, channel_start, channels, 1)
    local_weights = lax.dynamic_slice_in_dim(weights_all, channel_start, channels, 0)
    prior = jnp.einsum("jf,jsc->fsc", local_basis, coeffs, precision=lax.Precision.HIGHEST)
    new_gains = gain_update(normals, dual, prior, local_weights)
    partial_moments = jnp.einsum(
        "jf,fsc->jsc", local_weighted, new_gains + dual, precision=lax.Precision.HIGHEST
    )
    moments = lax.psum(partial_moments, "sub")
    new_coeffs = poly_solve(factor_lower, moments)
    consensus = jnp.einsum("jf,jsc->fsc", local_basis, new_coeffs, precision=lax.Precision.HIGHEST)
    new_dual = dual + new_gains - consensus
    return (new_gains, new_dual, new_coeffs)


def solution(mesh):
    placed = (
        P("sub", "bl", None),
        P(None, "sub", "bl"),
        P(None, "bl"),
        P("sub", "bl", None),
        P("sub", "bl", None),
        P(None, "bl", None),
        P(),
    )
    return jax.shard_map(
        shards,
        mesh=mesh,
        in_specs=placed,
        out_specs=(P("sub", "bl", None), P("sub", "bl", None), P(None, "bl", None)),
        check_vma=False,
    )
```

profile of v0, /device:TPU:2, one launch (start us, length us, event | category | flops | bytes accessed | tf_op | source)
XLA Modules:
  0.0 416.7 jit_solution(10042783867628545038)
XLA Ops:
  7.2 1.6 copy.43
  8.9 6.5 %copy.45 = bf16[8,2048,128]{1,2,0:T(8,128)(2,1)} copy(bf16[8,2048,128]{2,1,0:T(8,128)(2,1)} %param.9) | data formatting | bytes 8388608 | tf_op args[0]
  15.5 6.5 %convert_element_type.38 = f32[8,2048,128]{1,2,0:T(8,128)} convert(bf16[8,2048,128]{1,2,0:T(8,128)(2,1)} %copy.45) | non-fusion elementwise | flops 2097152 | bytes 12582912 | tf_op jit(solution)/shard_map/convert_element_type | solution.py:26
  22.0 45.5 %all-gather.2.cloned.1.call-done = f32[8,512,128]{2,0,1:T(8,128)} async-done(((f32[8,32,128]{2,0,1:T(8,128)}), f32[8,512,128]{2,0,1:T(8,128)}) %all-gather.2.cloned.1.call-update) | async-done | bytes 2097168 | tf_op jit(solution)/shard_map/all_gather | solution.py:83
  67.5 17.3 %gather_fusion = f32[2048,8,128]{2,1,0:T(8,128)} fusion(f32[8,512,128]{2,0,1:T(8,128)} %all-gather.2.cloned.1.call-done, s32[2048]{0:T(1024)S(1)} %fusion.16), kind=kCustom, calls=%fused_computation.clone | custom fusion | bytes 16785408 | tf_op jit(solution)/shard_map/jit(_take)/gather | solution.py:22
  84.8 9.5 %copy.44 = f32[2048,8,128]{0,2,1:T(8,128)} copy(f32[2048,8,128]{2,1,0:T(8,128)} %gather_fusion) | data formatting | bytes 16777216 | tf_op jit(solution)/shard_map/jit(_take)/gather | solution.py:22
  94.3 17.6 %gather_fusion.1 = f32[2048,8,128]{2,1,0:T(8,128)} fusion(f32[8,512,128]{2,0,1:T(8,128)S(1)} %copy-done.1, s32[2048]{0:T(1024)S(1)} %fusion.17), kind=kCustom, calls=%fused_computation.1.clone | custom fusion | bytes 16785408 | tf_op jit(solution)/shard_map/jit(_take)/gather | solution.py:23
  111.9 9.4 %copy.46 = f32[2048,8,128]{0,2,1:T(8,128)} copy(f32[2048,8,128]{2,1,0:T(8,128)} %gather_fusion.1) | data formatting | bytes 16777216 | tf_op jit(solution)/shard_map/jit(_take)/gather | solution.py:23
  121.3 9.3 %select_bitcast_fusion = (f32[8,2048,128]{1,2,0:T(8,128)}, f32[8,2048,128]{1,2,0:T(8,128)S(1)}) fusion(f32[2048,8,128]{0,2,1:T(8,128)} %copy.46, pred[2048]{0:T(1024)(128)(4,1)S(1)} %compare_and_fusion, f32[2048,8,128]{0,2,1:T(8,128)} %copy.44, pred[2048]{0:T(1024)(128)(4,1)S(1)} %compare_and_fusion.1), kind=kLoop, calls=%fused_computation.2 | loop fusion | flops 4194304 | bytes 33558528 | tf_op jit(solution)/shard_map/jit(_take)/select_n | solution.py:23
  130.6 9.5 %fusion.33 = (f32[8,2048]{1,0:T(8,128)S(1)}, f32[8,2048,64]{1,2,0:T(8,128)S(1)}, f32[8,2048,64]{1,2,0:T(8,128)}, f32[8,2048,64]{1,2,0:T(8,128)}) fusion(f32[8,2048,128]{1,2,0:T(8,128)S(1)} %get-tuple-element.54, f32[8,2048,128]{1,2,0:T(8,128)} %get-tuple-element.53, f32[8,2048,128]{1,2,0:T(8,128)} %convert_element_type.38), kind=kLoop, calls=%fused_computation.84 | loop fusion | flops 10469376 | bytes 37814272 | tf_op jit(solution)/shard_map/reduce_sum | solution.py:32
  140.1 7.5 %fusion.34 = (f32[8,2048]{1,0:T(8,128)S(1)}, f32[8,2048,64]{1,2,0:T(8,128)}) fusion(f32[8,2048,64]{1,2,0:T(8,128)} %get-tuple-element.25, f32[8,2048,128]{1,2,0:T(8,128)S(1)} %get-tuple-element.54, f32[8,2048,64]{1,2,0:T(8,128)} %get-tuple-element.26), kind=kLoop, calls=%fused_computation.85 | loop fusion | flops 4177920 | bytes 21037056 | tf_op jit(solution)/shard_map/reduce_sum | solution.py:33
  147.6 10.1 %add_convert_fusion.1 = (bf16[8,2048,64]{1,2,0:T(8,128)(2,1)}, f32[8,2048,64]{1,2,0:T(8,128)}, f32[8,2048,64]{1,2,0:T(8,128)}) fusion(f32[8,2048,64]{1,2,0:T(8,128)} %get-tuple-element.28, f32[8,2048,64]{1,2,0:T(8,128)S(1)} %get-tuple-element.24, f32[8,2048]{1,0:T(8,128)S(1)} %get-tuple-element.34, f32[8,2048]{1,0:T(8,128)S(1)} %get-tuple-element.33, ...), kind=kLoop, calls=%fused_computation.8 | loop fusion | flops 12582912 | bytes 35782656 | tf_op jit(solution)/shard_map/convert
  157.8 6.0 %add_convert_fusion = bf16[8,2048,64]{1,2,0:T(8,128)(2,1)} fusion(f32[8,2048,64]{1,2,0:T(8,128)} %get-tuple-element.22, f32[8,2048,64]{1,2,0:T(8,128)} %get-tuple-element.21), kind=kLoop, calls=%fused_computation.6 | loop fusion | flops 4194304 | bytes 10485760 | tf_op jit(solution)/shard_map/convert.2
  164.3 8.0 %add_convert_fusion.3 = (bf16[8,2048,64]{1,2,0:T(8,128)(2,1)S(1)}, bf16[8,2048,64]{1,2,0:T(8,128)(2,1)S(1)}, bf16[8,2048,64]{1,2,0:T(8,128)(2,1)}, bf16[8,2048,64]{1,2,0:T(8,128)(2,1)}) fusion(f32[8,2048,64]{1,2,0:T(8,128)S(1)} %copy-done.3, f32[8,2048,64]{1,2,0:T(8,128)S(1)} %copy-done.2, f32[8,2048,64]{1,2,0:T(8,128)} %get-tuple-element.28, ...), kind=kLoop, calls=%fused_computation.14 | loop fusion | flops 18874368 | bytes 33685504 | tf_op jit(solution)/shard_map/convert.3
  172.4 3.6 pad_maximum_fusion.1
  175.9 3.5 fusion.1
  179.5 5.1 %pad_maximum_fusion = bf16[8,2048,192]{1,2,0:T(8,128)(2,1)S(1)} fusion(bf16[8,2048,64]{1,2,0:T(8,128)(2,1)S(1)} %copy-done.4, bf16[8,2048,64]{1,2,0:T(8,128)(2,1)S(1)} %get-tuple-element.30, bf16[8,2048,64]{1,2,0:T(8,128)(2,1)S(1)} %get-tuple-element.29), kind=kLoop, calls=%fused_computation.4 | loop fusion | flops 18874368 | bytes 12582912 | tf_op jit(solution)/shard_map/concatenate | solution.py:38
  184.6 3.5 fusion
  188.1 0.7 add.119
  188.8 2.3 copy.57
  193.3 79.8 %reduce-scatter.4.cloned.1.call-done = f32[32,1536]{1,0:T(8,128)} async-done(((f32[512,1536]{1,0:T(8,128)}), f32[32,1536]{1,0:T(8,128)}) %reduce-scatter.4.cloned.1.call-update) | async-done | bytes 196624
  273.2 1.2 copy.58
  278.8 123.8 %all-reduce.2.cloned.1.call-done = f32[4,32,128]{2,1,0:T(8,128)} async-done(((f32[4,32,128]{2,1,0:T(8,128)}), f32[4,32,128]{2,1,0:T(8,128)}) %all-reduce.2.cloned.1.call-update) | async-done | bytes 65552 | tf_op jit(solution)/shard_map/psum | solution.py:117
  402.6 6.5 %subtract_divide_fusion = (f32[1,32,128]{2,1,0:T(8,128)S(1)}, f32[1,32,128]{2,1,0:T(8,128)S(1)}, f32[1,32,128]{2,1,0:T(8,128)S(1)}, f32[1,32,128]{2,1,0:T(8,128)S(1)}) fusion(f32[]{:T(128)} %bitcast.25, f32[]{:T(128)} %bitcast.22, f32[]{:T(128)} %bitcast.19, f32[]{:T(128)} %bitcast.18, f32[4,32,128]{2,1,0:T(8,128)} %all-reduce.2.cloned.1.call-done, ...), kind=kLoop, calls=%fused_computation.49 | loop fusion | flops 126976 | bytes 131112 | tf_op jit(solution)/shard_map/div | solution.py:78
  (54 shorter events, 7.0 us)
Async XLA Ops:
  7.2 267.6 %copy-start = (f32[4,32,128]{2,1,0:T(8,128)S(1)}, f32[4,32,128]{2,1,0:T(8,128)}, u32[]{:S(2)}) copy-start(f32[4,32,128]{2,1,0:T(8,128)} %param.14) | copy-start | bytes 196612
  7.2 60.3 %all-gather.2.cloned.1.call-start = ((), (), s32[]{:S(2)}) async-start(), calls=%async_computation.1 | async-start | bytes 2228224 | tf_op jit(solution)/shard_map/all_gather | solution.py:83
  8.9 264.3 %reduce-scatter.4.cloned.1.call-start = ((), (), s32[]{:S(2)}) async-start(), calls=%async_computation.3 | async-start | bytes 3342336
  15.5 6.5 %copy-start.8 = (s32[2,2048]{1,0:T(2,128)S(1)}, s32[2,2048]{1,0:T(2,128)}, u32[]{:S(2)}) copy-start(s32[2,2048]{1,0:T(2,128)} %param.11) | copy-start | bytes 49156
  84.8 9.5 %copy-start.1 = (f32[8,512,128]{2,0,1:T(8,128)S(1)}, f32[8,512,128]{2,0,1:T(8,128)}, u32[]{:S(2)}) copy-start(f32[8,512,128]{2,0,1:T(8,128)} %all-gather.2.cloned.1.call-done) | copy-start | bytes 6291460
  140.1 7.5 %copy-start.7 = (f32[2,8,2048]{2,1,0:T(8,128)S(1)}, f32[2,8,2048]{2,1,0:T(8,128)}, u32[]{:S(2)}) copy-start(f32[2,8,2048]{2,1,0:T(8,128)} %param.10) | copy-start | bytes 393220
  157.8 6.0 %copy-start.2 = (f32[8,2048,64]{1,2,0:T(8,128)S(1)}, f32[8,2048,64]{1,2,0:T(8,128)}, u32[]{:S(2)}) copy-start(f32[8,2048,64]{1,2,0:T(8,128)} %get-tuple-element.25) | copy-start | bytes 12582916
  157.8 6.5 %copy-start.3 = (f32[8,2048,64]{1,2,0:T(8,128)S(1)}, f32[8,2048,64]{1,2,0:T(8,128)}, u32[]{:S(2)}) copy-start(f32[8,2048,64]{1,2,0:T(8,128)} %get-tuple-element.26) | copy-start | bytes 12582916
  175.9 3.5 copy-start.4
  188.8 2.4 copy-start.9
  191.2 83.6 %copy-start.5 = (f32[8,32,128]{2,1,0:T(8,128)S(1)}, f32[8,32,128]{2,1,0:T(8,128)}, u32[]{:S(2)}) copy-start(f32[8,32,128]{2,1,0:T(8,128)} %param.13) | copy-start | bytes 393220
  191.2 211.4 %all-reduce.2.cloned.1.call-start = ((), (), s32[]{:S(2)}) async-start(), calls=%async_computation.2 | async-start | bytes 131072 | tf_op jit(solution)/shard_map/psum | solution.py:117
  409.1 1.1 copy-start.6
Sparse Core Ops, SparseCore 0:
  11.3 56.1 all-gather.1
  191.3 81.8 reduce-scatter.3
  276.4 126.1 all-reduce.1
where the time goes:
time: 417 us
  waiting for transfers between devices  249 us (60%)
  other arithmetic  74.6 us (18%)
  local copies, waits for them, and re-layouts  69.3 us (17%)
  between operations  15.3 us (4%)
  matrix products  8.22 us (2%)
    psum x1, waiting for transfers between devices, shards(): moments = lax.psum(partial_moments, 'sub')  124 us
    unnamed x4, waiting for transfers between devices  79.9 us
    all_gather x1, waiting for transfers between devices, shards(): full_gains = lax.all_gather(gains, 'bl', axis=1, tiled=True)  45.5 us
    gather x2, local copies, waits for them, and re-layouts, channel_terms(): far = jnp.take(gain_table, right_end, axis=-2)  27 us
    gather x2, local copies, waits for them, and re-layouts, channel_terms(): near = jnp.take(gain_table, lower_edge, axis=-2)  26.8 us
    another operation x3, other arithmetic  24.2 us
    unnamed x26, local copies, waits for them, and re-layouts  13.6 us
    reduce_sum x1, other arithmetic, channel_terms(): resid_re = vis_re - jnp.sum(model_re, axis=-1)  9.51 us
  transfers between devices with their start and end apart: 3, of which 3 were waited for; matrix products, arithmetic and copies ran while one was open for 4% of the time, Pallas kernels for 0%

commit v1 on v0

v1 whole, which is shorter than its diff:
```python
import functools
import math

import jax
import jax.numpy as jnp
from jax import lax
from jax.experimental import pallas as pl
from jax.experimental.pallas import tpu as pltpu
from jax.sharding import PartitionSpec as P

MESH = pl.DeviceIdType.MESH
BF = jnp.bfloat16
F32 = jnp.float32
PAIRS = 4
STATIONS = 512
HALF = 256
OWN = 32
BASE = 2048
CHIPS = 8
SUBS = 16
TERMS = 4
BLOCK = 512


def bernstein(position):
    degree = TERMS - 1
    rest = 1.0 - position
    out = []
    for order in range(TERMS):
        value = jnp.full_like(position, float(math.comb(degree, order)))
        for _ in range(order):
            value = value * position
        for _ in range(degree - order):
            value = value * rest
        out.append(value)
    return out


def swap_halves(value):
    return pltpu.roll(value, 64, 1)


def kernel(
    coh_hbm, vis_hbm, gains_ref, dual_ref, coeffs_ref, stations_ref, pen_row, pen_smem,
    ng_ref, nd_ref, nc_ref,
    coh, vis, wide, cols, colb, hot_p, hot_q, hot_pt, hot_qt, mix,
    table, split, terms_p, terms_q, sums, core_in, chip_sum, chip_in,
    mom, mom_in, mom_all, fac,
    load_sem, ag_send, ag_recv, relay_send, relay_recv, core_send, core_recv,
    rs_send, rs_recv, m_send, m_recv, r_send, r_recv,
):
    k = lax.axis_index("sub")
    i = lax.axis_index("bl")
    m = i // 2
    c = i % 2
    other = (k, m * 2 + (1 - c))

    def chip_peer(d):
        return (k, lax.rem(m + d, CHIPS) * 2 + c)

    def sub_peer(d):
        return (lax.rem(k + d, SUBS), i)

    load_vis = pltpu.make_async_copy(vis_hbm, vis, load_sem.at[0])
    load_vis.start()
    load_coh = pltpu.make_async_copy(coh_hbm, coh, load_sem.at[1])
    load_coh.start()

    barrier = pltpu.get_barrier_semaphore()
    pl.semaphore_signal(barrier, inc=1, device_id=other, device_id_type=MESH)
    for d in range(1, CHIPS):
        pl.semaphore_signal(barrier, inc=1, device_id=chip_peer(d), device_id_type=MESH)
    for d in range(1, SUBS):
        pl.semaphore_signal(barrier, inc=1, device_id=sub_peer(d), device_id_type=MESH)

    low = lax.broadcasted_iota(jnp.int32, (OWN, 128), 1) < 64
    own_row = pl.multiple_of(c * HALF + m * OWN, OWN)
    for j in range(PAIRS):
        first, second = gains_ref[2 * j], gains_ref[2 * j + 1]
        table[j, pl.ds(own_row, OWN), 0:128] = jnp.where(low, first, swap_halves(second))
        table[j, pl.ds(own_row, OWN), 128:256] = jnp.where(low, swap_halves(first), second)

    pl.semaphore_wait(barrier, 1 + (CHIPS - 1) + (SUBS - 1))

    for j in range(PAIRS):
        for d in range(1, CHIPS):
            rows = table.at[j, pl.ds(own_row, OWN)]
            pltpu.make_async_remote_copy(
                src_ref=rows, dst_ref=rows, send_sem=ag_send.at[j], recv_sem=ag_recv.at[j],
                device_id=chip_peer(d), device_id_type=MESH,
            ).start()

    raw = stations_ref[...]
    spot = ((raw >> 5) & 1) * HALF + (raw >> 6) * OWN + (raw & 31)
    load_vis.wait()
    spot_f = spot.astype(F32)
    seen = vis[...].reshape(16, BASE)
    coarse = seen.astype(BF).astype(F32)
    wide[...] = jnp.zeros_like(wide)
    wide[0:16] = coarse
    wide[16:32] = seen - coarse
    wide[32:34] = spot_f

    def turn(t, _):
        at = pl.ds(pl.multiple_of(t * 128, 128), 128)
        piece = wide[:, at].T
        cols[at, :] = piece
        colb[at, :] = piece.astype(BF)
        for hot, col in ((hot_p, 32), (hot_q, 33)):
            lane = lax.broadcasted_iota(jnp.int32, (128, STATIONS), 1).astype(F32)
            hot[at, :] = jnp.where(piece[:, col:col + 1] == lane, 1.0, 0.0).astype(BF)
        return 0

    lax.fori_loop(0, BASE // 128, turn, 0)

    def turn_t(t, _):
        at = pl.ds(pl.multiple_of(t * 32, 32), 32)
        row = (lax.broadcasted_iota(jnp.int32, (32, BASE), 0) + t * 32).astype(F32)
        hot_pt[at, :] = jnp.where(wide[32:33, :] == row, 1.0, 0.0).astype(BF)
        hot_qt[at, :] = jnp.where(wide[33:34, :] == row, 1.0, 0.0).astype(BF)
        return 0

    lax.fori_loop(0, STATIONS // 32, turn_t, 0)

    out_lane = lax.broadcasted_iota(jnp.int32, (128, 256), 1)
    in_row = lax.broadcasted_iota(jnp.int32, (128, 256), 0)
    in_lane = lax.broadcasted_iota(jnp.int32, (256, 256), 0)
    out_wide = lax.broadcasted_iota(jnp.int32, (256, 256), 1)
    for j in range(PAIRS):
        want = (out_lane // 128) * 8 + 2 * j + (out_lane // 64) % 2
        hit = (in_row < 32) & (in_row % 16 == want)
        minus = jnp.where(in_lane // 64 == out_wide // 64, -1.0, 0.0).astype(BF)
        mix[j, 0:256] = minus
        mix[j, 256:512] = minus
        mix[j, 512:640] = jnp.where(hit, 1.0, 0.0).astype(BF)

    channel = lax.broadcasted_iota(jnp.int32, (1, 128), 1).astype(F32)
    rows_b = bernstein((channel + 0.5) / 128.0)
    weight_row = 4.0 * pen_row[...].astype(F32)
    lower = {}
    for r in range(TERMS):
        for q in range(r + 1):
            value = jnp.sum(weight_row * rows_b[r] * rows_b[q], axis=1, keepdims=True)
            for s in range(q):
                value = value - lower[r, s] * lower[q, s]
            lower[r, q] = jnp.sqrt(value) if r == q else value / lower[q, q]
            fac[4 * r + q:4 * r + q + 1, :] = jnp.broadcast_to(lower[r, q], (1, 128))

    load_coh.wait()

    def relay(j):
        got = table.at[j, pl.ds(0, (CHIPS - 1) * OWN)]
        pltpu.make_async_remote_copy(
            src_ref=got, dst_ref=got, send_sem=ag_send.at[j], recv_sem=ag_recv.at[j],
            device_id=other, device_id_type=MESH,
        ).wait_recv()
        half = table.at[j, pl.ds(pl.multiple_of(c * HALF, HALF), HALF)]
        pltpu.make_async_remote_copy(
            src_ref=half, dst_ref=half, send_sem=relay_send.at[j], recv_sem=relay_recv.at[j],
            device_id=other, device_id_type=MESH,
        ).start()

    def relay_copy(j):
        half = table.at[j, pl.ds(pl.multiple_of(c * HALF, HALF), HALF)]
        return pltpu.make_async_remote_copy(
            src_ref=half, dst_ref=half, send_sem=relay_send.at[j], recv_sem=relay_recv.at[j],
            device_id=other, device_id_type=MESH,
        )

    def core_copy(j):
        return pltpu.make_async_remote_copy(
            src_ref=sums.at[j, pl.ds(pl.multiple_of((1 - c) * HALF, HALF), HALF)],
            dst_ref=core_in.at[j], send_sem=core_send.at[j], recv_sem=core_recv.at[j],
            device_id=other, device_id_type=MESH,
        )

    def to_owners(j):
        core_copy(j).wait_recv()
        chip_sum[j] = sums[j, pl.ds(pl.multiple_of(c * HALF, HALF), HALF)] + core_in[j]
        for d in range(1, CHIPS):
            owner = lax.rem(m + d, CHIPS)
            pltpu.make_async_remote_copy(
                src_ref=chip_sum.at[j, pl.ds(pl.multiple_of(owner * OWN, OWN), OWN)],
                dst_ref=chip_in.at[j, d - 1], send_sem=rs_send.at[j], recv_sem=rs_recv.at[j],
                device_id=chip_peer(d), device_id_type=MESH,
            ).start()

    def all_in(j):
        return pltpu.make_async_remote_copy(
            src_ref=chip_in.at[j], dst_ref=chip_in.at[j], send_sem=rs_send.at[j],
            recv_sem=rs_recv.at[j], device_id=other, device_id_type=MESH,
        )

    wide_low = lax.broadcasted_iota(jnp.int32, (BLOCK, 128), 1) < 64

    relay(0)
    for j in range(PAIRS):
        relay_copy(j).wait_recv()
        whole = table[j]
        high = whole.astype(BF)
        split[0:512] = high
        split[512:1024] = (whole - high.astype(F32)).astype(BF)

        def block(b, _, j=j):
            at = pl.ds(pl.multiple_of(b * BLOCK, BLOCK), BLOCK)
            hp = hot_p[at, :]
            hq = hot_q[at, :]
            near = jnp.dot(jnp.concatenate([hp, hp], 1), split[...], preferred_element_type=F32)
            far = jnp.dot(jnp.concatenate([hq, hq], 1), split[...], preferred_element_type=F32)
            c0 = coh[2 * j, at, :].astype(F32)
            c1 = coh[2 * j + 1, at, :].astype(F32)
            cr = jnp.where(wide_low, c0, swap_halves(c1))
            ci = jnp.where(wide_low, swap_halves(c0), c1)
            nr, ni = near[:, 0:128], near[:, 128:256]
            fr, fi = far[:, 0:128], far[:, 128:256]
            hr = cr * fr + ci * fi
            hi = ci * fr - cr * fi
            mr = nr * hr - ni * hi
            mi = nr * hi + ni * hr
            mrh, mih = mr.astype(BF), mi.astype(BF)
            mrl = (mr - mrh.astype(F32)).astype(BF)
            mil = (mi - mih.astype(F32)).astype(BF)
            resid = jnp.dot(
                jnp.concatenate([mrh, mih, mrl, mil, colb[at, :]], 1), mix[j],
                preferred_element_type=F32,
            )
            tr = resid[:, 0:128] + mr
            ti = resid[:, 128:256] + mi
            er = cr * nr - ci * ni
            ei = cr * ni + ci * nr
            terms_p[at, 0:128] = (tr * hr + ti * hi).astype(BF)
            terms_p[at, 128:256] = (ti * hr - tr * hi).astype(BF)
            terms_p[at, 256:384] = (hr * hr + hi * hi).astype(BF)
            terms_q[at, 0:128] = (tr * er + ti * ei).astype(BF)
            terms_q[at, 128:256] = (tr * ei - ti * er).astype(BF)
            terms_q[at, 256:384] = (er * er + ei * ei).astype(BF)
            return 0

        lax.fori_loop(0, BASE // BLOCK, block, 0)
        if j + 1 < PAIRS:
            relay(j + 1)
        if j > 0:
            to_owners(j - 1)

        def scatter(r, _, j=j):
            at = pl.ds(pl.multiple_of(r * 256, 256), 256)
            sums[j, at, :] = jnp.dot(
                hot_pt[at, :], terms_p[...], preferred_element_type=F32
            ) + jnp.dot(hot_qt[at, :], terms_q[...], preferred_element_type=F32)
            return 0

        lax.fori_loop(0, STATIONS // 256, scatter, 0)
        core_copy(j).start()
    to_owners(PAIRS - 1)

    co = [coeffs_ref[t] for t in range(TERMS)]
    co_re = [jnp.where(low, v, swap_halves(v)) for v in co]
    co_im = [jnp.where(low, swap_halves(v), v) for v in co]
    half_lane = lax.broadcasted_iota(jnp.int32, (1, 128), 1)
    total = [jnp.zeros((OWN, 128), F32) for _ in range(TERMS)]
    basis_of = []
    for j in range(PAIRS):
        all_in(j).wait_recv()
        normal = chip_sum[j, pl.ds(pl.multiple_of(m * OWN, OWN), OWN)]
        for d in range(CHIPS - 1):
            normal = normal + chip_in[j, d]
        f0 = k * 8 + 2 * j
        p0 = jnp.full((1, 128), pen_smem[f0], jnp.int32)
        p1 = jnp.full((1, 128), pen_smem[f0 + 1], jnp.int32)
        w0 = 4.0 * p0.astype(F32)
        w1 = 4.0 * p1.astype(F32)
        spot0 = (jnp.full((1, 128), f0, jnp.int32).astype(F32) + 0.5) / 128.0
        spot1 = (jnp.full((1, 128), f0 + 1, jnp.int32).astype(F32) + 0.5) / 128.0
        b0, b1 = bernstein(spot0), bernstein(spot1)
        basis_of += [b0, b1]
        weight = jnp.where(half_lane < 64, w0, w1)
        both = [jnp.where(half_lane < 64, u, v) for u, v in zip(b0, b1)]
        d0, d1 = dual_ref[2 * j], dual_ref[2 * j + 1]
        dual_re = jnp.where(low, d0, swap_halves(d1))
        dual_im = jnp.where(low, swap_halves(d0), d1)
        prior_re = sum(both[t] * co_re[t] for t in range(TERMS))
        prior_im = sum(both[t] * co_im[t] for t in range(TERMS))
        below = normal[:, 256:384] + weight
        gain_re = (normal[:, 0:128] + weight * (prior_re - dual_re)) / below
        gain_im = (normal[:, 128:256] + weight * (prior_im - dual_im)) / below
        g0 = jnp.where(low, gain_re, swap_halves(gain_im))
        g1 = jnp.where(low, swap_halves(gain_re), gain_im)
        ng_ref[2 * j] = g0
        ng_ref[2 * j + 1] = g1
        for t in range(TERMS):
            total[t] = total[t] + (w0 * b0[t]) * (g0 + d0) + (w1 * b1[t]) * (g1 + d1)

    for t in range(TERMS):
        mom[4 * t:4 * t + 4] = total[t].reshape(4, 8, 128)
    for d in range(1, SUBS):
        pltpu.make_async_remote_copy(
            src_ref=mom.at[lax.rem(k + d, SUBS)], dst_ref=mom_in.at[d - 1],
            send_sem=m_send, recv_sem=m_recv, device_id=sub_peer(d), device_id_type=MESH,
        ).start()
    m_all = pltpu.make_async_remote_copy(
        src_ref=mom_in, dst_ref=mom_in, send_sem=m_send, recv_sem=m_recv,
        device_id=other, device_id_type=MESH,
    )
    m_all.wait_recv()
    tile = mom[k]
    for d in range(SUBS - 1):
        tile = tile + mom_in[d]
    mom_all[k] = tile
    for d in range(1, SUBS):
        pltpu.make_async_remote_copy(
            src_ref=mom_all.at[k], dst_ref=mom_all.at[k],
            send_sem=r_send, recv_sem=r_recv, device_id=sub_peer(d), device_id_type=MESH,
        ).start()
    r_all = pltpu.make_async_remote_copy(
        src_ref=mom_all.at[pl.ds(0, SUBS - 1)], dst_ref=mom_all.at[pl.ds(0, SUBS - 1)],
        send_sem=r_send, recv_sem=r_recv, device_id=other, device_id_type=MESH,
    )
    r_all.wait_recv()

    low_of = lambda r, q: fac[4 * r + q:4 * r + q + 1, :]
    forward = []
    for r in range(TERMS):
        value = mom_all[4 * r:4 * r + 4].reshape(OWN, 128)
        for q in range(r):
            value = value - low_of(r, q) * forward[q]
        forward.append(value / low_of(r, r))
    back = [None] * TERMS
    for r in range(TERMS - 1, -1, -1):
        value = forward[r]
        for q in range(r + 1, TERMS):
            value = value - low_of(q, r) * back[q]
        back[r] = value / low_of(r, r)
        nc_ref[r] = back[r]
    for f in range(2 * PAIRS):
        agreed = sum(basis_of[f][t] * back[t] for t in range(TERMS))
        nd_ref[f] = dual_ref[f] + ng_ref[f] - agreed

    for j in range(PAIRS):
        sent = table.at[j, pl.ds(0, (CHIPS - 1) * OWN)]
        pltpu.make_async_remote_copy(
            src_ref=sent, dst_ref=sent, send_sem=ag_send.at[j], recv_sem=ag_recv.at[j],
            device_id=other, device_id_type=MESH,
        ).wait_send()
        relay_copy(j).wait_send()
        core_copy(j).wait_send()
        all_in(j).wait_send()
    m_all.wait_send()
    r_all.wait_send()


def step(coherency, visibility, stations, gains, dual, coeffs, penalty):
    vmem = pl.BlockSpec(memory_space=pltpu.VMEM)
    hbm = pl.BlockSpec(memory_space=pl.ANY)
    dma = pltpu.SemaphoreType.DMA
    return pl.pallas_call(
        kernel,
        out_shape=(
            jax.ShapeDtypeStruct(gains.shape, F32),
            jax.ShapeDtypeStruct(gains.shape, F32),
            jax.ShapeDtypeStruct(coeffs.shape, F32),
        ),
        in_specs=[hbm, hbm, vmem, vmem, vmem, vmem, vmem, pl.BlockSpec(memory_space=pltpu.SMEM)],
        out_specs=(vmem, vmem, vmem),
        scratch_shapes=[
            pltpu.VMEM((8, BASE, 128), BF),
            pltpu.VMEM((2, 8, BASE), F32),
            pltpu.VMEM((128, BASE), F32),
            pltpu.VMEM((BASE, 128), F32),
            pltpu.VMEM((BASE, 128), BF),
            pltpu.VMEM((BASE, STATIONS), BF),
            pltpu.VMEM((BASE, STATIONS), BF),
            pltpu.VMEM((STATIONS, BASE), BF),
            pltpu.VMEM((STATIONS, BASE), BF),
            pltpu.VMEM((PAIRS, 640, 256), BF),
            pltpu.VMEM((PAIRS, STATIONS, 256), F32),
            pltpu.VMEM((2 * STATIONS, 256), BF),
            pltpu.VMEM((BASE, 384), BF),
            pltpu.VMEM((BASE, 384), BF),
            pltpu.VMEM((PAIRS, STATIONS, 384), F32),
            pltpu.VMEM((PAIRS, HALF, 384), F32),
            pltpu.VMEM((PAIRS, HALF, 384), F32),
            pltpu.VMEM((PAIRS, CHIPS - 1, OWN, 384), F32),
            pltpu.VMEM((SUBS, 8, 128), F32),
            pltpu.VMEM((SUBS - 1, 8, 128), F32),
            pltpu.VMEM((SUBS, 8, 128), F32),
            pltpu.VMEM((16, 128), F32),
            dma((2,)),
            dma((PAIRS,)), dma((PAIRS,)),
            dma((PAIRS,)), dma((PAIRS,)),
            dma((PAIRS,)), dma((PAIRS,)),
            dma((PAIRS,)), dma((PAIRS,)),
            dma(()), dma(()), dma(()), dma(()),
        ],
        compiler_params=pltpu.CompilerParams(
            collective_id=0, has_side_effects=True, vmem_limit_bytes=56 * 1024 * 1024
        ),
    )(coherency, visibility, gains, dual, coeffs, stations, penalty.reshape(1, 128), penalty)


def solution(mesh):
    placed = (
        P("sub", "bl", None),
        P(None, "sub", "bl"),
        P(None, "bl"),
        P("sub", "bl", None),
        P("sub", "bl", None),
        P(None, "bl", None),
        P(),
    )
    return jax.shard_map(
        step,
        mesh=mesh,
        in_specs=placed,
        out_specs=(P("sub", "bl", None), P("sub", "bl", None), P(None, "bl", None)),
        check_vma=False,
    )
```

time: 417 us -> 78.6 us (0.19)
  the two profiles are of different devices: /device:TPU:2 before, /device:TPU:16 now
where the time goes in v1:
time: 78.6 us; the launch traced here: 78.4 us
  Pallas kernels  73.1 us (93%)
  local copies, waits for them, and re-layouts  4.61 us (6%)
    pallas_call x1, Pallas kernels, step(): pl.pallas_call(kernel, out_shape=(jax.ShapeDtypeStruct(gains.shape, F32),...  73.1 us
    unnamed x3, local copies, waits for them, and re-layouts  4.61 us

profile of v1, /device:TPU:16, one launch (start us, length us, event | category | flops | bytes accessed | tf_op | source)
XLA Modules:
  0.0 78.4 jit_solution(14119069243839130662)
XLA Ops:
  0.6 73.1 %shard_map.94 = (f32[8,32,128]{2,1,0:T(8,128)}, f32[8,32,128]{2,1,0:T(8,128)}, f32[4,32,128]{2,1,0:T(8,128)}) custom-call(bf16[8,2048,128]{2,1,0:T(8,128)(2,1)} %coh_hbm.1, f32[2,8,2048]{2,1,0:T(8,128)} %vis_hbm.1, f32[8,32,128]{2,1,0:T(8,128)} %gains_ref.1, f32[8,32,128]{2,1,0:T(8,128)} %dual_ref.1, f32[4,32,128]{2,1,0:T(8,128)} %coeffs_ref.1, ...), custom_call_target="tpu_custom_call" | custom-call | tf_op jit(solution)/shard_map/pallas_call | solution.py:355
  73.8 1.6 %copy.13 = f32[8,32,128]{2,1,0:T(8,128)} copy(f32[8,32,128]{2,1,0:T(8,128)} %get-tuple-element.6) | data formatting | bytes 262144
  75.3 1.6 %copy.14 = f32[8,32,128]{2,1,0:T(8,128)} copy(f32[8,32,128]{2,1,0:T(8,128)} %get-tuple-element.7) | data formatting | bytes 262144
  76.9 1.5 %copy.15 = f32[4,32,128]{2,1,0:T(8,128)} copy(f32[4,32,128]{2,1,0:T(8,128)} %get-tuple-element.8) | data formatting | bytes 131072

commit v2 on v1

v2 whole, which is shorter than its diff:
```python
import functools
import math

import jax
import jax.numpy as jnp
from jax import lax
from jax.experimental import pallas as pl
from jax.experimental.pallas import tpu as pltpu
from jax.sharding import PartitionSpec as P

MESH = pl.DeviceIdType.MESH
BF = jnp.bfloat16
F32 = jnp.float32
PAIRS = 4
STATIONS = 512
HALF = 256
OWN = 32
BASE = 2048
CHIPS = 8
SUBS = 16
TERMS = 4
BLOCK = 512
CHIP_HOPS = ((2, 1), (2, 0), (1, 1), (3, 1), (0, 1), (1, 0), (3, 0))
SUB_HOPS = (
    (1, 4), (0, 4), (1, 3), (1, 5), (0, 3), (0, 5), (1, 2), (1, 6),
    (0, 2), (0, 6), (1, 1), (1, 7), (0, 1), (0, 7), (1, 0),
)


def bernstein(position):
    degree = TERMS - 1
    rest = 1.0 - position
    out = []
    for order in range(TERMS):
        value = jnp.full_like(position, float(math.comb(degree, order)))
        for _ in range(order):
            value = value * position
        for _ in range(degree - order):
            value = value * rest
        out.append(value)
    return out


def swap_halves(value):
    return pltpu.roll(value, 64, 1)


def kernel(
    coh_hbm, vis_hbm, gains_hbm, dual_hbm, coeffs_hbm, stations_hbm, pen_row, pen_smem,
    ng_hbm, mom_hbm, fac_hbm,
    coh, vis, gains_ref, dual_ref, coeffs_ref, stations_ref, ng_ref,
    wide, colb, hot, hot_pt, hot_qt, mix,
    table, split, pulled0, pulled1, terms_p, terms_q, sums, core_in, chip_sum, chip_in,
    mom, mom_in, mom_all, fac,
    ready, load_sem, out_sem, ag_send, ag_recv, relay_send, relay_recv, core_send, core_recv,
    rs_send, rs_recv, m_send, m_recv, r_send, r_recv,
):
    k = lax.axis_index("sub")
    i = lax.axis_index("bl")
    m = i // 2
    c = i % 2
    other = (k, m * 2 + (1 - c))

    def chip_at(hop):
        return lax.rem(m // 2 + hop[0], 4) * 2 + lax.rem(m + hop[1], 2)

    def chip_peer(hop):
        return (k, chip_at(hop) * 2 + c)

    def sub_at(hop):
        return lax.rem(k // 8 + hop[0], 2) * 8 + lax.rem(k + hop[1], 8)

    def sub_peer(hop):
        return (sub_at(hop), i)

    barrier = pltpu.get_barrier_semaphore()
    pl.semaphore_signal(barrier, inc=1, device_id=other, device_id_type=MESH)
    for hop in CHIP_HOPS:
        pl.semaphore_signal(barrier, inc=1, device_id=chip_peer(hop), device_id_type=MESH)
    above, below = sub_peer((0, 1)), sub_peer((0, 7))
    for near in (above, below, sub_peer((1, 0))):
        pl.semaphore_signal(barrier, inc=1, device_id=near, device_id_type=MESH)

    load_gains = pltpu.make_async_copy(gains_hbm, gains_ref, load_sem.at[2])
    load_gains.start()
    load_stations = pltpu.make_async_copy(stations_hbm, stations_ref, load_sem.at[3])
    load_stations.start()
    load_vis = pltpu.make_async_copy(vis_hbm, vis, load_sem.at[0])
    load_vis.start()
    load_coh = pltpu.make_async_copy(coh_hbm, coh, load_sem.at[1])
    load_coh.start()
    load_dual = pltpu.make_async_copy(dual_hbm, dual_ref, load_sem.at[4])
    load_dual.start()
    load_coeffs = pltpu.make_async_copy(coeffs_hbm, coeffs_ref, load_sem.at[5])
    load_coeffs.start()

    low = lax.broadcasted_iota(jnp.int32, (OWN, 128), 1) < 64
    load_gains.wait()
    own_row = pl.multiple_of(c * HALF + m * OWN, OWN)
    for j in range(PAIRS):
        first, second = gains_ref[2 * j], gains_ref[2 * j + 1]
        table[j, pl.ds(own_row, OWN), 0:128] = jnp.where(low, first, swap_halves(second))
        table[j, pl.ds(own_row, OWN), 128:256] = jnp.where(low, swap_halves(first), second)

    pl.semaphore_wait(barrier, 1 + (CHIPS - 1) + 3)

    def spread(j):
        for hop in CHIP_HOPS:
            rows = table.at[j, pl.ds(own_row, OWN)]
            pltpu.make_async_remote_copy(
                src_ref=rows, dst_ref=rows, send_sem=ag_send.at[j], recv_sem=ag_recv.at[j],
                device_id=chip_peer(hop), device_id_type=MESH,
            ).start()

    def heard(j):
        for near in (above, below):
            pl.semaphore_signal(ready.at[j], inc=1, device_id=near, device_id_type=MESH)

    spread(0)
    heard(0)

    load_stations.wait()
    raw = stations_ref[...]
    spot = ((raw >> 5) & 1) * HALF + (raw >> 6) * OWN + (raw & 31)
    load_vis.wait()
    spot_f = spot.astype(F32)
    seen = vis[...].reshape(16, BASE)
    coarse = seen.astype(BF).astype(F32)
    wide[...] = jnp.zeros_like(wide)
    wide[0:16] = coarse
    wide[16:32] = seen - coarse
    wide[32:34] = spot_f

    def turn(t, _):
        at = pl.ds(pl.multiple_of(t * 128, 128), 128)
        piece = wide[:, at].T
        colb[at, :] = piece.astype(BF)
        lane = lax.broadcasted_iota(jnp.int32, (128, STATIONS), 1).astype(F32)
        per = BLOCK // 128
        for end in range(2):
            to = pl.ds(pl.multiple_of(((t // per) * 2 + end) * BLOCK + (t % per) * 128, 128), 128)
            hot[to, :] = jnp.where(piece[:, 32 + end:33 + end] == lane, 1.0, 0.0).astype(BF)
        return 0

    lax.fori_loop(0, BASE // 128, turn, 0)

    def turn_t(t, _):
        at = pl.ds(pl.multiple_of(t * 32, 32), 32)
        row = (lax.broadcasted_iota(jnp.int32, (32, BASE), 0) + t * 32).astype(F32)
        hot_pt[at, :] = jnp.where(wide[32:33, :] == row, 1.0, 0.0).astype(BF)
        hot_qt[at, :] = jnp.where(wide[33:34, :] == row, 1.0, 0.0).astype(BF)
        return 0

    lax.fori_loop(0, STATIONS // 32, turn_t, 0)

    spread(1)
    out_lane = lax.broadcasted_iota(jnp.int32, (128, 256), 1)
    in_row = lax.broadcasted_iota(jnp.int32, (128, 256), 0)
    in_lane = lax.broadcasted_iota(jnp.int32, (256, 256), 0)
    out_wide = lax.broadcasted_iota(jnp.int32, (256, 256), 1)
    for j in range(PAIRS):
        want = (out_lane // 128) * 8 + 2 * j + (out_lane // 64) % 2
        hit = (in_row < 32) & (in_row % 16 == want)
        minus = jnp.where(in_lane // 64 == out_wide // 64, -1.0, 0.0).astype(BF)
        mix[j, 0:256] = minus
        mix[j, 256:512] = minus
        mix[j, 512:640] = jnp.where(hit, 1.0, 0.0).astype(BF)

    channel = lax.broadcasted_iota(jnp.int32, (1, 128), 1).astype(F32)
    rows_b = bernstein((channel + 0.5) / 128.0)
    weight_row = 4.0 * pen_row[...].astype(F32)
    lower = {}
    for r in range(TERMS):
        for q in range(r + 1):
            value = jnp.sum(weight_row * rows_b[r] * rows_b[q], axis=1, keepdims=True)
            for s in range(q):
                value = value - lower[r, s] * lower[q, s]
            lower[r, q] = jnp.sqrt(value) if r == q else value / lower[q, q]
            fac[4 * r + q:4 * r + q + 1, :] = jnp.broadcast_to(lower[r, q], (1, 128))

    load_coh.wait()

    def relay(j):
        got = table.at[j, pl.ds(0, (CHIPS - 1) * OWN)]
        pltpu.make_async_remote_copy(
            src_ref=got, dst_ref=got, send_sem=ag_send.at[j], recv_sem=ag_recv.at[j],
            device_id=other, device_id_type=MESH,
        ).wait_recv()
        half = table.at[j, pl.ds(pl.multiple_of(c * HALF, HALF), HALF)]
        pltpu.make_async_remote_copy(
            src_ref=half, dst_ref=half, send_sem=relay_send.at[j], recv_sem=relay_recv.at[j],
            device_id=other, device_id_type=MESH,
        ).start()

    def relay_copy(j):
        half = table.at[j, pl.ds(pl.multiple_of(c * HALF, HALF), HALF)]
        return pltpu.make_async_remote_copy(
            src_ref=half, dst_ref=half, send_sem=relay_send.at[j], recv_sem=relay_recv.at[j],
            device_id=other, device_id_type=MESH,
        )

    def core_copy(j):
        return pltpu.make_async_remote_copy(
            src_ref=sums.at[j, pl.ds(pl.multiple_of((1 - c) * HALF, HALF), HALF)],
            dst_ref=core_in.at[j], send_sem=core_send.at[j], recv_sem=core_recv.at[j],
            device_id=other, device_id_type=MESH,
        )

    def to_owners(j):
        core_copy(j).wait_recv()
        chip_sum[j] = sums[j, pl.ds(pl.multiple_of(c * HALF, HALF), HALF)] + core_in[j]
        for slot, hop in enumerate(CHIP_HOPS):
            owner = chip_at(hop)
            pltpu.make_async_remote_copy(
                src_ref=chip_sum.at[j, pl.ds(pl.multiple_of(owner * OWN, OWN), OWN)],
                dst_ref=chip_in.at[j, slot], send_sem=rs_send.at[j], recv_sem=rs_recv.at[j],
                device_id=chip_peer(hop), device_id_type=MESH,
            ).start()

    def all_in(j):
        return pltpu.make_async_remote_copy(
            src_ref=chip_in.at[j], dst_ref=chip_in.at[j], send_sem=rs_send.at[j],
            recv_sem=rs_recv.at[j], device_id=other, device_id_type=MESH,
        )

    wide_low = lax.broadcasted_iota(jnp.int32, (BLOCK, 128), 1) < 64

    relay(0)
    spread(2)

    def gather(b, pulled):
        both = hot[b * 2 * BLOCK:(b + 1) * 2 * BLOCK, :]
        pulled[...] = jnp.dot(
            jnp.concatenate([both, both], 1), split[...], preferred_element_type=F32
        )

    def combine(j, b, pulled):
        at = slice(b * BLOCK, (b + 1) * BLOCK)
        c0 = coh[2 * j, at, :].astype(F32)
        c1 = coh[2 * j + 1, at, :].astype(F32)
        cr = jnp.where(wide_low, c0, swap_halves(c1))
        ci = jnp.where(wide_low, swap_halves(c0), c1)
        nr, ni = pulled[0:BLOCK, 0:128], pulled[0:BLOCK, 128:256]
        fr, fi = pulled[BLOCK:2 * BLOCK, 0:128], pulled[BLOCK:2 * BLOCK, 128:256]
        hr = cr * fr + ci * fi
        hi = ci * fr - cr * fi
        mr = nr * hr - ni * hi
        mi = nr * hi + ni * hr
        mrh, mih = mr.astype(BF), mi.astype(BF)
        mrl = (mr - mrh.astype(F32)).astype(BF)
        mil = (mi - mih.astype(F32)).astype(BF)
        resid = jnp.dot(
            jnp.concatenate([mrh, mih, mrl, mil, colb[at, :]], 1), mix[j],
            preferred_element_type=F32,
        )
        tr = resid[:, 0:128] + mr
        ti = resid[:, 128:256] + mi
        er = cr * nr - ci * ni
        ei = cr * ni + ci * nr
        terms_p[at, 0:128] = (tr * hr + ti * hi).astype(BF)
        terms_p[at, 128:256] = (ti * hr - tr * hi).astype(BF)
        terms_p[at, 256:384] = (hr * hr + hi * hi).astype(BF)
        terms_q[at, 0:128] = (tr * er + ti * ei).astype(BF)
        terms_q[at, 128:256] = (tr * ei - ti * er).astype(BF)
        terms_q[at, 256:384] = (er * er + ei * ei).astype(BF)

    def scatter(rows, at):
        return jnp.dot(
            hot_pt[rows, at], terms_p[at, :], preferred_element_type=F32
        ) + jnp.dot(hot_qt[rows, at], terms_q[at, :], preferred_element_type=F32)

    blocks = BASE // BLOCK
    early = slice(0, BASE - BLOCK)
    late = slice(BASE - BLOCK, BASE)
    theirs = pl.ds(pl.multiple_of((1 - c) * HALF, HALF), HALF)
    mine = pl.ds(pl.multiple_of(c * HALF, HALF), HALF)

    def pair(j, _):
        relay_copy(j).wait_recv()
        whole = table[j]
        high = whole.astype(BF)
        split[0:512] = high
        split[512:1024] = (whole - high.astype(F32)).astype(BF)
        pulled = (pulled0, pulled1)
        gather(0, pulled[0])
        for b in range(blocks - 1):
            gather(b + 1, pulled[(b + 1) % 2])
            combine(j, b, pulled[b % 2])
            if b == 0:
                pl.when(j > 0)(lambda: to_owners(j - 1))
                pl.when(j == 0)(lambda: spread(3))

        pl.when(j + 1 < PAIRS)(lambda: relay(j + 1))
        pl.semaphore_wait(ready.at[j], 2)
        pl.when(j + 1 < PAIRS)(lambda: heard(j + 1))
        sums[j, theirs, :] = scatter(theirs, early)
        sums[j, mine, :] = scatter(mine, early)
        combine(j, blocks - 1, pulled[(blocks - 1) % 2])
        sums[j, theirs, :] += scatter(theirs, late)
        core_copy(j).start()
        sums[j, mine, :] += scatter(mine, late)
        return 0

    lax.fori_loop(0, PAIRS, pair, 0)
    to_owners(PAIRS - 1)

    load_dual.wait()
    load_coeffs.wait()
    co = [coeffs_ref[t] for t in range(TERMS)]
    co_re = [jnp.where(low, v, swap_halves(v)) for v in co]
    co_im = [jnp.where(low, swap_halves(v), v) for v in co]
    half_lane = lax.broadcasted_iota(jnp.int32, (1, 128), 1)
    total = [jnp.zeros((OWN, 128), F32) for _ in range(TERMS)]
    for j in range(PAIRS):
        all_in(j).wait_recv()
        normal = chip_sum[j, pl.ds(pl.multiple_of(m * OWN, OWN), OWN)]
        for d in range(CHIPS - 1):
            normal = normal + chip_in[j, d]
        f0 = k * 8 + 2 * j
        p0 = jnp.full((1, 128), pen_smem[f0], jnp.int32)
        p1 = jnp.full((1, 128), pen_smem[f0 + 1], jnp.int32)
        w0 = 4.0 * p0.astype(F32)
        w1 = 4.0 * p1.astype(F32)
        spot0 = (jnp.full((1, 128), f0, jnp.int32).astype(F32) + 0.5) / 128.0
        spot1 = (jnp.full((1, 128), f0 + 1, jnp.int32).astype(F32) + 0.5) / 128.0
        b0, b1 = bernstein(spot0), bernstein(spot1)
        weight = jnp.where(half_lane < 64, w0, w1)
        both = [jnp.where(half_lane < 64, u, v) for u, v in zip(b0, b1)]
        d0, d1 = dual_ref[2 * j], dual_ref[2 * j + 1]
        dual_re = jnp.where(low, d0, swap_halves(d1))
        dual_im = jnp.where(low, swap_halves(d0), d1)
        prior_re = sum(both[t] * co_re[t] for t in range(TERMS))
        prior_im = sum(both[t] * co_im[t] for t in range(TERMS))
        under = normal[:, 256:384] + weight
        gain_re = (normal[:, 0:128] + weight * (prior_re - dual_re)) / under
        gain_im = (normal[:, 128:256] + weight * (prior_im - dual_im)) / under
        g0 = jnp.where(low, gain_re, swap_halves(gain_im))
        g1 = jnp.where(low, swap_halves(gain_re), gain_im)
        ng_ref[2 * j] = g0
        ng_ref[2 * j + 1] = g1
        for t in range(TERMS):
            total[t] = total[t] + (w0 * b0[t]) * (g0 + d0) + (w1 * b1[t]) * (g1 + d1)

    out_gains = pltpu.make_async_copy(ng_ref, ng_hbm, out_sem.at[0])
    out_gains.start()
    out_fac = pltpu.make_async_copy(fac, fac_hbm, out_sem.at[1])
    out_fac.start()
    for t in range(TERMS):
        mom[4 * t:4 * t + 4] = total[t].reshape(4, 8, 128)
    for slot, hop in enumerate(SUB_HOPS):
        pltpu.make_async_remote_copy(
            src_ref=mom.at[sub_at(hop)], dst_ref=mom_in.at[slot],
            send_sem=m_send, recv_sem=m_recv, device_id=sub_peer(hop), device_id_type=MESH,
        ).start()
    m_all = pltpu.make_async_remote_copy(
        src_ref=mom_in, dst_ref=mom_in, send_sem=m_send, recv_sem=m_recv,
        device_id=other, device_id_type=MESH,
    )
    m_all.wait_recv()
    tile = mom[k]
    for d in range(SUBS - 1):
        tile = tile + mom_in[d]
    mom_all[k] = tile
    for hop in SUB_HOPS:
        pltpu.make_async_remote_copy(
            src_ref=mom_all.at[k], dst_ref=mom_all.at[k],
            send_sem=r_send, recv_sem=r_recv, device_id=sub_peer(hop), device_id_type=MESH,
        ).start()
    r_all = pltpu.make_async_remote_copy(
        src_ref=mom_all.at[pl.ds(0, SUBS - 1)], dst_ref=mom_all.at[pl.ds(0, SUBS - 1)],
        send_sem=r_send, recv_sem=r_recv, device_id=other, device_id_type=MESH,
    )
    r_all.wait_recv()

    out_mom = pltpu.make_async_copy(mom_all, mom_hbm, out_sem.at[2])
    out_mom.start()

    for j in range(PAIRS):
        sent = table.at[j, pl.ds(0, (CHIPS - 1) * OWN)]
        pltpu.make_async_remote_copy(
            src_ref=sent, dst_ref=sent, send_sem=ag_send.at[j], recv_sem=ag_recv.at[j],
            device_id=other, device_id_type=MESH,
        ).wait_send()
        relay_copy(j).wait_send()
        core_copy(j).wait_send()
        all_in(j).wait_send()
    m_all.wait_send()
    r_all.wait_send()
    out_gains.wait()
    out_fac.wait()
    out_mom.wait()


def finish(ng_ref, dual_ref, mom_all, fac, ng_out, nd_ref, nc_ref):
    k = lax.axis_index("sub")
    low_of = lambda r, q: fac[4 * r + q:4 * r + q + 1, :]
    forward = []
    for r in range(TERMS):
        value = mom_all[4 * r:4 * r + 4].reshape(OWN, 128)
        for q in range(r):
            value = value - low_of(r, q) * forward[q]
        forward.append(value / low_of(r, r))
    back = [None] * TERMS
    for r in range(TERMS - 1, -1, -1):
        value = forward[r]
        for q in range(r + 1, TERMS):
            value = value - low_of(q, r) * back[q]
        back[r] = value / low_of(r, r)
        nc_ref[r] = back[r]
    for f in range(2 * PAIRS):
        spot = (jnp.full((1, 128), k * 8 + f, jnp.int32).astype(F32) + 0.5) / 128.0
        basis = bernstein(spot)
        agreed = sum(basis[t] * back[t] for t in range(TERMS))
        gain = ng_ref[f]
        ng_out[f] = gain
        nd_ref[f] = dual_ref[f] + gain - agreed


def step(coherency, visibility, stations, gains, dual, coeffs, penalty):
    vmem = pl.BlockSpec(memory_space=pltpu.VMEM)
    hbm = pl.BlockSpec(memory_space=pl.ANY)
    dma = pltpu.SemaphoreType.DMA
    gained, moments, factor = pl.pallas_call(
        kernel,
        out_shape=(
            jax.ShapeDtypeStruct(gains.shape, F32),
            jax.ShapeDtypeStruct((SUBS, 8, 128), F32),
            jax.ShapeDtypeStruct((16, 128), F32),
        ),
        in_specs=[hbm, hbm, hbm, hbm, hbm, hbm, vmem, pl.BlockSpec(memory_space=pltpu.SMEM)],
        out_specs=(hbm, hbm, hbm),
        scratch_shapes=[
            pltpu.VMEM((8, BASE, 128), BF),
            pltpu.VMEM((2, 8, BASE), F32),
            pltpu.VMEM((8, OWN, 128), F32),
            pltpu.VMEM((8, OWN, 128), F32),
            pltpu.VMEM((TERMS, OWN, 128), F32),
            pltpu.VMEM((2, BASE), jnp.int32),
            pltpu.VMEM((8, OWN, 128), F32),
            pltpu.VMEM((128, BASE), F32),
            pltpu.VMEM((BASE, 128), BF),
            pltpu.VMEM((2 * BASE, STATIONS), BF),
            pltpu.VMEM((STATIONS, BASE), BF),
            pltpu.VMEM((STATIONS, BASE), BF),
            pltpu.VMEM((PAIRS, 640, 256), BF),
            pltpu.VMEM((PAIRS, STATIONS, 256), F32),
            pltpu.VMEM((2 * STATIONS, 256), BF),
            pltpu.VMEM((2 * BLOCK, 256), F32),
            pltpu.VMEM((2 * BLOCK, 256), F32),
            pltpu.VMEM((BASE, 384), BF),
            pltpu.VMEM((BASE, 384), BF),
            pltpu.VMEM((PAIRS, STATIONS, 384), F32),
            pltpu.VMEM((PAIRS, HALF, 384), F32),
            pltpu.VMEM((PAIRS, HALF, 384), F32),
            pltpu.VMEM((PAIRS, CHIPS - 1, OWN, 384), F32),
            pltpu.VMEM((SUBS, 8, 128), F32),
            pltpu.VMEM((SUBS - 1, 8, 128), F32),
            pltpu.VMEM((SUBS, 8, 128), F32),
            pltpu.VMEM((16, 128), F32),
            pltpu.SemaphoreType.REGULAR((PAIRS,)), dma((6,)), dma((3,)),
            dma((PAIRS,)), dma((PAIRS,)),
            dma((PAIRS,)), dma((PAIRS,)),
            dma((PAIRS,)), dma((PAIRS,)),
            dma((PAIRS,)), dma((PAIRS,)),
            dma(()), dma(()), dma(()), dma(()),
        ],
        compiler_params=pltpu.CompilerParams(
            collective_id=0, has_side_effects=True, vmem_limit_bytes=56 * 1024 * 1024
        ),
    )(coherency, visibility, gains, dual, coeffs, stations, penalty.reshape(1, 128), penalty)
    return pl.pallas_call(
        finish,
        out_shape=(
            jax.ShapeDtypeStruct(gains.shape, F32),
            jax.ShapeDtypeStruct(gains.shape, F32),
            jax.ShapeDtypeStruct(coeffs.shape, F32),
        ),
        in_specs=[vmem] * 4,
        out_specs=(vmem,) * 3,
    )(gained, dual, moments, factor)


def solution(mesh):
    placed = (
        P("sub", "bl", None),
        P(None, "sub", "bl"),
        P(None, "bl"),
        P("sub", "bl", None),
        P("sub", "bl", None),
        P(None, "bl", None),
        P(),
    )
    return jax.shard_map(
        step,
        mesh=mesh,
        in_specs=placed,
        out_specs=(P("sub", "bl", None), P("sub", "bl", None), P(None, "bl", None)),
        check_vma=False,
    )
```

time: 78.6 us -> 66.4 us (0.84)
  the two profiles are of different devices: /device:TPU:16 before, /device:TPU:2 now
where the time goes in v2:
time: 66.4 us; the launch traced here: 65.8 us
  Pallas kernels  65.2 us (98%)
    pallas_call x1, Pallas kernels, step(): pl.pallas_call(kernel, out_shape=(jax.ShapeDtypeStruct(gains.shape, F32),...  63.4 us
    pallas_call x1, Pallas kernels, step(): pl.pallas_call(finish, out_shape=(jax.ShapeDtypeStruct(gains.shape, F32),...  1.73 us

profile of v2, /device:TPU:2, one launch (start us, length us, event | category | flops | bytes accessed | tf_op | source)
XLA Modules:
  0.0 65.8 jit_solution(1921517877011011562)
XLA Ops:
  0.6 63.4 %shard_map.94 = (f32[8,32,128]{2,1,0:T(8,128)}, f32[16,8,128]{2,1,0:T(8,128)}, f32[16,128]{1,0:T(8,128)}) custom-call(bf16[8,2048,128]{2,1,0:T(8,128)(2,1)} %coh_hbm.1, f32[2,8,2048]{2,1,0:T(8,128)} %vis_hbm.1, f32[8,32,128]{2,1,0:T(8,128)} %gains_hbm.1, f32[8,32,128]{2,1,0:T(8,128)} %dual_ref.1, f32[4,32,128]{2,1,0:T(8,128)} %coeffs_hbm.1, ...), custom_call_target="tpu_custom_call" | custom-call | tf_op jit(solution)/shard_map/pallas_call | solution.py:423
  64.1 1.7 %shard_map.95 = (f32[8,32,128]{2,1,0:T(8,128)}, f32[8,32,128]{2,1,0:T(8,128)}, f32[4,32,128]{2,1,0:T(8,128)}) custom-call(f32[8,32,128]{2,1,0:T(8,128)} %get-tuple-element.6.ng_ref, f32[8,32,128]{2,1,0:T(8,128)} %dual_ref.1, f32[16,8,128]{2,1,0:T(8,128)} %get-tuple-element.7.mom_all, f32[16,128]{1,0:T(8,128)} %get-tuple-element.8.fac), custom_call_target="tpu_custom_call" | custom-call | tf_op jit(solution)/shard_map/pallas_call | solution.py:471

commit v3 on v2

--- a/solution.py
+++ b/solution.py
@@ -11,6 +11,8 @@
 MESH = pl.DeviceIdType.MESH
 BF = jnp.bfloat16
 F32 = jnp.float32
+F8 = jnp.float8_e5m2
+FINE = 256.0
 PAIRS = 4
 STATIONS = 512
 HALF = 256
@@ -50,7 +52,7 @@
     ng_hbm, mom_hbm, fac_hbm,
     coh, vis, gains_ref, dual_ref, coeffs_ref, stations_ref, ng_ref,
     wide, colb, hot, hot_pt, hot_qt, mix,
-    table, split, pulled0, pulled1, terms_p, terms_q, sums, core_in, chip_sum, chip_in,
+    table, split, fine, hot_fine, pulled0, pulled1, terms_p, terms_q, sums, core_in, chip_sum, chip_in,
     mom, mom_in, mom_all, fac,
     ready, load_sem, out_sem, ag_send, ag_recv, relay_send, relay_recv, core_send, core_recv,
     rs_send, rs_recv, m_send, m_recv, r_send, r_recv,
@@ -139,7 +141,9 @@
         per = BLOCK // 128
         for end in range(2):
             to = pl.ds(pl.multiple_of(((t // per) * 2 + end) * BLOCK + (t % per) * 128, 128), 128)
-            hot[to, :] = jnp.where(piece[:, 32 + end:33 + end] == lane, 1.0, 0.0).astype(BF)
+            match = piece[:, 32 + end:33 + end] == lane
+            hot[to, :] = jnp.where(match, 1.0, 0.0).astype(BF)
+            hot_fine[to, :] = jnp.where(match, 1.0 / FINE, 0.0).astype(F8)
         return 0
 
     lax.fori_loop(0, BASE // 128, turn, 0)
@@ -229,9 +233,9 @@
     spread(2)
 
     def gather(b, pulled):
-        both = hot[b * 2 * BLOCK:(b + 1) * 2 * BLOCK, :]
-        pulled[...] = jnp.dot(
-            jnp.concatenate([both, both], 1), split[...], preferred_element_type=F32
+        at = slice(b * 2 * BLOCK, (b + 1) * 2 * BLOCK)
+        pulled[...] = jnp.dot(hot[at, :], split[...], preferred_element_type=F32) + jnp.dot(
+            hot_fine[at, :], fine[...], preferred_element_type=F32
         )
 
     def combine(j, b, pulled):
@@ -279,8 +283,8 @@
         relay_copy(j).wait_recv()
         whole = table[j]
         high = whole.astype(BF)
-        split[0:512] = high
-        split[512:1024] = (whole - high.astype(F32)).astype(BF)
+        split[...] = high
+        fine[...] = ((whole - high.astype(F32)) * FINE).astype(F8)
         pulled = (pulled0, pulled1)
         gather(0, pulled[0])
         for b in range(blocks - 1):
@@ -293,8 +297,7 @@
         pl.when(j + 1 < PAIRS)(lambda: relay(j + 1))
         pl.semaphore_wait(ready.at[j], 2)
         pl.when(j + 1 < PAIRS)(lambda: heard(j + 1))
-        sums[j, theirs, :] = scatter(theirs, early)
-        sums[j, mine, :] = scatter(mine, early)
+        sums[j] = scatter(slice(0, STATIONS), early)
         combine(j, blocks - 1, pulled[(blocks - 1) % 2])
         sums[j, theirs, :] += scatter(theirs, late)
         core_copy(j).start()
@@ -444,7 +447,9 @@
             pltpu.VMEM((STATIONS, BASE), BF),
             pltpu.VMEM((PAIRS, 640, 256), BF),
             pltpu.VMEM((PAIRS, STATIONS, 256), F32),
-            pltpu.VMEM((2 * STATIONS, 256), BF),
+            pltpu.VMEM((STATIONS, 256), BF),
+            pltpu.VMEM((STATIONS, 256), F8),
+            pltpu.VMEM((2 * BASE, STATIONS), F8),
             pltpu.VMEM((2 * BLOCK, 256), F32),
             pltpu.VMEM((2 * BLOCK, 256), F32),
             pltpu.VMEM((BASE, 384), BF),

time: 66.4 us -> 65.3 us (0.983)
  Pallas kernels: 65.2 us -> 63.7 us
    pallas_call x1, Pallas kernels: 63.4 us -> 62 us  [step(): pl.pallas_call(kernel, out_shape=(jax.ShapeDtypeStruct(gains.shape, F32),...]
where the time goes in v3:
time: 65.3 us; the launch traced here: 64.4 us
  Pallas kernels  63.7 us (98%)
    pallas_call x1, Pallas kernels, step(): pl.pallas_call(kernel, out_shape=(jax.ShapeDtypeStruct(gains.shape, F32),...  62 us
    pallas_call x1, Pallas kernels, step(): pl.pallas_call(finish, out_shape=(jax.ShapeDtypeStruct(gains.shape, F32),...  1.73 us

profile of v3, /device:TPU:2, one launch (start us, length us, event | category | flops | bytes accessed | tf_op | source)
XLA Modules:
  0.0 64.4 jit_solution(2496873263084269884)
XLA Ops:
  0.6 62.0 %shard_map.94 = (f32[8,32,128]{2,1,0:T(8,128)}, f32[16,8,128]{2,1,0:T(8,128)}, f32[16,128]{1,0:T(8,128)}) custom-call(bf16[8,2048,128]{2,1,0:T(8,128)(2,1)} %coh_hbm.1, f32[2,8,2048]{2,1,0:T(8,128)} %vis_hbm.1, f32[8,32,128]{2,1,0:T(8,128)} %gains_hbm.1, f32[8,32,128]{2,1,0:T(8,128)} %dual_ref.1, f32[4,32,128]{2,1,0:T(8,128)} %coeffs_hbm.1, ...), custom_call_target="tpu_custom_call" | custom-call | tf_op jit(solution)/shard_map/pallas_call | solution.py:426
  62.7 1.7 %shard_map.95 = (f32[8,32,128]{2,1,0:T(8,128)}, f32[8,32,128]{2,1,0:T(8,128)}, f32[4,32,128]{2,1,0:T(8,128)}) custom-call(f32[8,32,128]{2,1,0:T(8,128)} %get-tuple-element.6.ng_ref, f32[8,32,128]{2,1,0:T(8,128)} %dual_ref.1, f32[16,8,128]{2,1,0:T(8,128)} %get-tuple-element.7.mom_all, f32[16,128]{1,0:T(8,128)} %get-tuple-element.8.fac), custom_call_target="tpu_custom_call" | custom-call | tf_op jit(solution)/shard_map/pallas_call | solution.py:476

commit v4 on v3

--- a/solution.py
+++ b/solution.py
@@ -50,7 +50,7 @@
 def kernel(
     coh_hbm, vis_hbm, gains_hbm, dual_hbm, coeffs_hbm, stations_hbm, pen_row, pen_smem,
     ng_hbm, mom_hbm, fac_hbm,
-    coh, vis, gains_ref, dual_ref, coeffs_ref, stations_ref, ng_ref,
+    coh, packed, vis, gains_ref, dual_ref, coeffs_ref, stations_ref, ng_ref,
     wide, colb, hot, hot_pt, hot_qt, mix,
     table, split, fine, hot_fine, pulled0, pulled1, terms_p, terms_q, sums, core_in, chip_sum, chip_in,
     mom, mom_in, mom_all, fac,
@@ -183,6 +183,18 @@
             fac[4 * r + q:4 * r + q + 1, :] = jnp.broadcast_to(lower[r, q], (1, 128))
 
     load_coh.wait()
+    wide_low = lax.broadcasted_iota(jnp.int32, (256, 128), 1) < 64
+
+    def pack(t, _):
+        at = pl.ds(pl.multiple_of(t * 256, 256), 256)
+        for j in range(PAIRS):
+            c0 = coh[2 * j, at, :].astype(F32)
+            c1 = coh[2 * j + 1, at, :].astype(F32)
+            packed[j, at, 0:128] = jnp.where(wide_low, c0, swap_halves(c1)).astype(BF)
+            packed[j, at, 128:256] = jnp.where(wide_low, swap_halves(c0), c1).astype(BF)
+        return 0
+
+    lax.fori_loop(0, BASE // 256, pack, 0)
 
     def relay(j):
         got = table.at[j, pl.ds(0, (CHIPS - 1) * OWN)]
@@ -227,7 +239,6 @@
             recv_sem=rs_recv.at[j], device_id=other, device_id_type=MESH,
         )
 
-    wide_low = lax.broadcasted_iota(jnp.int32, (BLOCK, 128), 1) < 64
 
     relay(0)
     spread(2)
@@ -240,10 +251,8 @@
 
     def combine(j, b, pulled):
         at = slice(b * BLOCK, (b + 1) * BLOCK)
-        c0 = coh[2 * j, at, :].astype(F32)
-        c1 = coh[2 * j + 1, at, :].astype(F32)
-        cr = jnp.where(wide_low, c0, swap_halves(c1))
-        ci = jnp.where(wide_low, swap_halves(c0), c1)
+        cr = packed[j, at, 0:128].astype(F32)
+        ci = packed[j, at, 128:256].astype(F32)
         nr, ni = pulled[0:BLOCK, 0:128], pulled[0:BLOCK, 128:256]
         fr, fi = pulled[BLOCK:2 * BLOCK, 0:128], pulled[BLOCK:2 * BLOCK, 128:256]
         hr = cr * fr + ci * fi
@@ -434,6 +443,7 @@
         out_specs=(hbm, hbm, hbm),
         scratch_shapes=[
             pltpu.VMEM((8, BASE, 128), BF),
+            pltpu.VMEM((PAIRS, BASE, 256), BF),
             pltpu.VMEM((2, 8, BASE), F32),
             pltpu.VMEM((8, OWN, 128), F32),
             pltpu.VMEM((8, OWN, 128), F32),

time: 65.3 us -> 64.6 us (0.989)
  no operation moved by 1% of the time
where the time goes in v4:
time: 64.6 us; the launch traced here: 64 us
  Pallas kernels  63.3 us (98%)
    pallas_call x1, Pallas kernels, step(): pl.pallas_call(kernel, out_shape=(jax.ShapeDtypeStruct(gains.shape, F32),...  61.6 us
    pallas_call x1, Pallas kernels, step(): pl.pallas_call(finish, out_shape=(jax.ShapeDtypeStruct(gains.shape, F32),...  1.73 us

profile of v4, /device:TPU:2, one launch (start us, length us, event | category | flops | bytes accessed | tf_op | source)
XLA Modules:
  0.0 64.0 jit_solution(17536597660365737080)
XLA Ops:
  0.6 61.6 %shard_map.94 = (f32[8,32,128]{2,1,0:T(8,128)}, f32[16,8,128]{2,1,0:T(8,128)}, f32[16,128]{1,0:T(8,128)}) custom-call(bf16[8,2048,128]{2,1,0:T(8,128)(2,1)} %coh_hbm.1, f32[2,8,2048]{2,1,0:T(8,128)} %vis_hbm.1, f32[8,32,128]{2,1,0:T(8,128)} %gains_hbm.1, f32[8,32,128]{2,1,0:T(8,128)} %dual_ref.1, f32[4,32,128]{2,1,0:T(8,128)} %coeffs_hbm.1, ...), custom_call_target="tpu_custom_call" | custom-call | tf_op jit(solution)/shard_map/pallas_call | solution.py:435
  62.2 1.7 %shard_map.95 = (f32[8,32,128]{2,1,0:T(8,128)}, f32[8,32,128]{2,1,0:T(8,128)}, f32[4,32,128]{2,1,0:T(8,128)}) custom-call(f32[8,32,128]{2,1,0:T(8,128)} %get-tuple-element.6.ng_ref, f32[8,32,128]{2,1,0:T(8,128)} %dual_ref.1, f32[16,8,128]{2,1,0:T(8,128)} %get-tuple-element.7.mom_all, f32[16,128]{1,0:T(8,128)} %get-tuple-element.8.fac), custom_call_target="tpu_custom_call" | custom-call | tf_op jit(solution)/shard_map/pallas_call | solution.py:486

commit v5 on v4

--- a/solution.py
+++ b/solution.py
@@ -224,9 +224,13 @@
 
     def to_owners(j):
         core_copy(j).wait_recv()
-        chip_sum[j] = sums[j, pl.ds(pl.multiple_of(c * HALF, HALF), HALF)] + core_in[j]
-        for slot, hop in enumerate(CHIP_HOPS):
+        for slot, hop in enumerate(CHIP_HOPS + ((0, 0),)):
             owner = chip_at(hop)
+            rows = pl.ds(pl.multiple_of(owner * OWN, OWN), OWN)
+            ours = pl.ds(pl.multiple_of(c * HALF + owner * OWN, OWN), OWN)
+            chip_sum[j, rows] = sums[j, ours] + core_in[j, rows]
+            if hop == (0, 0):
+                continue
             pltpu.make_async_remote_copy(
                 src_ref=chip_sum.at[j, pl.ds(pl.multiple_of(owner * OWN, OWN), OWN)],
                 dst_ref=chip_in.at[j, slot], send_sem=rs_send.at[j], recv_sem=rs_recv.at[j],

time: 64.6 us -> 64.6 us (level)
  no operation moved by 1% of the time
where the time goes in v5:
time: 64.6 us; the launch traced here: 63.9 us
  Pallas kernels  63.2 us (98%)
    pallas_call x1, Pallas kernels, step(): pl.pallas_call(kernel, out_shape=(jax.ShapeDtypeStruct(gains.shape, F32),...  61.5 us
    pallas_call x1, Pallas kernels, step(): pl.pallas_call(finish, out_shape=(jax.ShapeDtypeStruct(gains.shape, F32),...  1.73 us

profile of v5, /device:TPU:2, one launch (start us, length us, event | category | flops | bytes accessed | tf_op | source)
XLA Modules:
  0.0 63.9 jit_solution(13926043824175803523)
XLA Ops:
  0.6 61.5 %shard_map.94 = (f32[8,32,128]{2,1,0:T(8,128)}, f32[16,8,128]{2,1,0:T(8,128)}, f32[16,128]{1,0:T(8,128)}) custom-call(bf16[8,2048,128]{2,1,0:T(8,128)(2,1)} %coh_hbm.1, f32[2,8,2048]{2,1,0:T(8,128)} %vis_hbm.1, f32[8,32,128]{2,1,0:T(8,128)} %gains_hbm.1, f32[8,32,128]{2,1,0:T(8,128)} %dual_ref.1, f32[4,32,128]{2,1,0:T(8,128)} %coeffs_hbm.1, ...), custom_call_target="tpu_custom_call" | custom-call | tf_op jit(solution)/shard_map/pallas_call | solution.py:439
  62.2 1.7 %shard_map.95 = (f32[8,32,128]{2,1,0:T(8,128)}, f32[8,32,128]{2,1,0:T(8,128)}, f32[4,32,128]{2,1,0:T(8,128)}) custom-call(f32[8,32,128]{2,1,0:T(8,128)} %get-tuple-element.6.ng_ref, f32[8,32,128]{2,1,0:T(8,128)} %dual_ref.1, f32[16,8,128]{2,1,0:T(8,128)} %get-tuple-element.7.mom_all, f32[16,128]{1,0:T(8,128)} %get-tuple-element.8.fac), custom_call_target="tpu_custom_call" | custom-call | tf_op jit(solution)/shard_map/pallas_call | solution.py:490
